TPU v7x, 32 devices: a whole 2x2x4 slice. The times are simulated.
32 devices in a mesh: ew: 2 (over y), ns: 16 (over z, x, core).
Axes of the slice: x: 2, y: 2, z: 4, core: 2. Of those that a mesh axis runs over, the one named last changes fastest.
Arguments:
- couplings: bfloat16 [2, 16, 16, 128, 2048], P('ew', 'ns'), may hold values from -0.125 to 0.125
- inverses: bfloat16 [2, 16, 16, 128, 128], P('ew', 'ns'), as said below
- pattern: int32 [2, 16, 16, 16], P('ew', 'ns'), may hold values 0 or 1
- counts: int32 [2, 16], P('ew', 'ns'), may hold values from 1 to 16, as said below
- basis: bfloat16 [2, 16, 128, 512], P('ew', 'ns'), may hold values from -0.25 to 0.25
Outputs:
- south_front: float32 [2, 16, 768, 768], P('ew', 'ns')
- west_front: float32 [2, 16, 256, 256], P('ew', 'ns')
- coarse: float32 [2, 16, 128, 128], P('ew', 'ns')
Inputs may be any that keep to these rules, and one draw needn't show every extreme that they name: `counts`: some subdomain has exactly 16 live block columns. `inverses`: each block is symmetric.
All inputs are finite; a program needn't handle non-finite values. No bound on the sum of `pattern` on one device may be relied on, other than what follows from the above.
Results may differ from a plain program's by a relative error of at most 0.0015.
Values may be sent and summed in bfloat16 or wider, within the bound.
A program may use at most 128 MiB of HBM per device.

v0:
```python
import jax
import jax.numpy as jnp
from jax import lax
from jax.sharding import PartitionSpec as P

B = 128
SN = 6
SE = 2


def from_behind(block, axis, distance):
    devices = range(lax.axis_size(axis))
    route = [(i - distance, i) for i in devices if i - distance in devices]
    return lax.ppermute(block, axis, route)


def solve_all(slabs, inverse):
    return jnp.einsum("kab,kbc->kac", inverse, slabs, preferred_element_type=jnp.float32).astype(
        jnp.bfloat16
    )


def edge_parts(slabs, solved, edges):
    results = []
    for edge in edges:
        slab = slabs[:, :, edge[0] : edge[0] + edge[1]]
        answer = solved[:, :, edge[0] : edge[0] + edge[1]]
        results.append(-jnp.einsum("kbi,kbj->ij", slab, answer, preferred_element_type=jnp.float32))
    return tuple(results)


def pass_edges(high_parts):
    from_west = from_behind(high_parts[0], "ew", 1)
    from_south = from_behind(high_parts[1], "ns", 1)
    return (from_west, from_south)


def shards(couplings, inverses, pattern, counts, basis):
    coupling = couplings[0, 0]
    inverse = inverses[0, 0]
    touched = pattern[0, 0]
    count = counts[0, 0]
    blocks_total = coupling.shape[0]
    north_start = SN * B
    west_start = 2 * SN * B
    east_start = west_start + SE * B
    south_edge = (0, SN * B)
    north_edge = (north_start, SN * B)
    west_edge = (west_start, SE * B)
    east_edge = (east_start, SE * B)
    columns = jnp.repeat(touched, B, axis=1)
    live = (jnp.arange(blocks_total, dtype=jnp.int32) < count).astype(jnp.int32)[:, None]
    keep = (columns * live).astype(jnp.bfloat16)
    masked = coupling * keep[:, None, :]
    high_edges = [east_edge, north_edge]
    solved = solve_all(masked, inverse)
    every_part = edge_parts(masked, solved, [south_edge, west_edge] + high_edges)
    low_parts = every_part[:2]
    from_west, from_south = pass_edges(every_part[2:])
    south_front = low_parts[0] + from_south
    west_front = low_parts[1] + from_west
    front_half = west_front.astype(jnp.bfloat16)
    row_basis = basis[0, 0]
    rank = row_basis.shape[0]
    edge_width = SE * B
    piece = lax.all_gather(front_half, "ew", axis=0, tiled=True)
    pieces = piece.shape[0] // edge_width
    columns_here = row_basis.reshape(rank, pieces, edge_width)
    fronts = piece.reshape(pieces, edge_width, edge_width)
    projected = jnp.einsum(
        "rnk,nkl->rnl", columns_here, fronts, preferred_element_type=jnp.float32
    ).astype(jnp.bfloat16)
    coarse = jnp.einsum("rnl,snl->rs", projected, columns_here, preferred_element_type=jnp.float32)
    return (south_front[None, None], west_front[None, None], coarse[None, None])


def solution(mesh):
    return jax.shard_map(
        shards,
        mesh=mesh,
        in_specs=(
            P("ew", "ns", None, None, None),
            P("ew", "ns", None, None, None),
            P("ew", "ns", None, None),
            P("ew", "ns"),
            P("ew", "ns", None, None),
        ),
        out_specs=(P("ew", "ns", None, None), P("ew", "ns", None, None), P("ew", "ns", None, None)),
        check_vma=False,
    )
```

profile of v0, /device:TPU:16, one launch (start us, length us, event | category | flops | bytes accessed | tf_op | source)
XLA Modules:
  0.0 69.7 jit_solution(10748349576370407610)
XLA Ops:
  0.6 0.0 copy-start
  0.6 0.0 copy-start.3
  0.7 12.3 %copy.8 = bf16[1,1,16,128,2048]{3,4,2,1,0:T(8,128)(2,1)} copy(bf16[1,1,16,128,2048]{4,3,2,1,0:T(8,128)(2,1)} %param.5) | data formatting | bytes 16777216 | tf_op args[0]
  13.7 0.0 copy-done.3
  13.7 0.1 broadcast_in_dim.14
  13.8 0.1 fusion.27
  13.9 6.4 %bitcast_multiply_fusion = bf16[16,128,2048]{1,2,0:T(8,128)(2,1)S(1)} fusion(bf16[1,1,16,128,2048]{3,4,2,1,0:T(8,128)(2,1)} %copy.8, bf16[16,2048]{1,0:T(8,128)(2,1)S(1)} %fusion.27), kind=kLoop, calls=%fused_computation | loop fusion | flops 4194304 | bytes 16842752 | tf_op jit(solution)/shard_map/mul | solution.py:54
  20.2 0.0 copy-done
  20.2 0.0 copy-start.1
  20.3 5.1 %convert_bitcast_fusion = bf16[16,128,2048]{1,2,0:T(8,128)(2,1)} fusion(bf16[16,128,2048]{1,2,0:T(8,128)(2,1)S(1)} %bitcast_multiply_fusion, bf16[1,1,16,128,128]{4,3,2,1,0:T(8,128)(2,1)S(1)} %copy-done), kind=kOutput, calls=%fused_computation.1 | convolution fusion | flops 1077936128 | bytes 17301504 | tf_op jit(solution)/shard_map/kab,kbc->kac/dot_general | solution.py:18
  25.3 0.0 copy-start.2
  25.3 6.2 %bitcast_negate_fusion = f32[768,768]{1,0:T(8,128)} fusion(bf16[16,128,2048]{1,2,0:T(8,128)(2,1)} %convert_bitcast_fusion, bf16[16,128,2048]{1,2,0:T(8,128)(2,1)S(1)} %bitcast_multiply_fusion), kind=kOutput, calls=%fused_computation.8 | convolution fusion | flops 2416508928 | bytes 8650752 | tf_op jit(solution)/shard_map/kbi,kbj->ij/dot_general | solution.py:28
  31.5 1.9 %collective-permute-start = (f32[768,768]{1,0:T(8,128)}, f32[768,768]{1,0:T(8,128)S(1)}, u32[]{:S(2)}, u32[]{:S(2)}) collective-permute-start(f32[768,768]{1,0:T(8,128)} %bitcast_negate_fusion), channel_id=1, source_target_pairs={{0,1},{1,2},{2,3},{3,4},{4,5},{5,6},{6,7},{7,8},{8,9},{9,10},{10,1... | collective-permute-start | bytes 7077896 | tf_op jit(solution)/shard_map/ppermute | solution.py:14
  33.4 0.0 copy-done.1
  33.5 2.4 %fusion.16 = f32[256,256]{1,0:T(8,128)} fusion(bf16[16,128,2048]{1,2,0:T(8,128)(2,1)} %convert_bitcast_fusion, bf16[16,128,2048]{1,2,0:T(8,128)(2,1)S(1)} %bitcast_multiply_fusion), kind=kOutput, calls=%fused_computation.13 | convolution fusion | flops 268500992 | bytes 2359296 | tf_op jit(solution)/shard_map/kbi,kbj->ij/dot_general | solution.py:28
  35.9 3.4 %collective-permute-start.1 = (f32[256,256]{1,0:T(8,128)}, f32[256,256]{1,0:T(8,128)S(1)}, u32[]{:S(2)}, u32[]{:S(2)}) collective-permute-start(f32[256,256]{1,0:T(8,128)} %fusion.16), channel_id=1, source_target_pairs={{0,16},{1,17},{2,18},{3,19},{4,20},{5,21},{6,22},{7,23},{8,24},{9,... | collective-permute-start | bytes 786440 | tf_op jit(solution)/shard_map/ppermute | solution.py:14
  39.3 0.0 copy-done.2
  39.3 6.4 %collective-permute-done.1 = f32[256,256]{1,0:T(8,128)S(1)} collective-permute-done((f32[256,256]{1,0:T(8,128)}, f32[256,256]{1,0:T(8,128)S(1)}, u32[]{:S(2)}, u32[]{:S(2)}) %collective-permute-start.1) | collective-permute-done | bytes 262176 | tf_op jit(solution)/shard_map/ppermute | solution.py:14
  45.7 2.7 %fusion.30 = (bf16[256,256]{1,0:T(8,128)(2,1)S(1)}, f32[256,256]{1,0:T(8,128)}) fusion(f32[256,256]{1,0:T(8,128)S(1)} %collective-permute-done.1, bf16[16,128,2048]{1,2,0:T(8,128)(2,1)} %convert_bitcast_fusion, bf16[16,128,2048]{1,2,0:T(8,128)(2,1)} %copy-done.1), kind=kOutput, calls=%fused_computation.30 | convolution fusion | flops 268632064 | bytes 2752512 | tf_op jit(solution)/shard_map/kbi,kbj->ij/dot_general | solution.py:28
  48.4 7.4 %all_gather.3 = bf16[512,256]{1,0:T(8,128)(2,1)S(1)} all-gather(bf16[256,256]{1,0:T(8,128)(2,1)S(1)} %get-tuple-element.3), channel_id=1, replica_groups=mesh['ew'=2,'ns'=16] {'ew'}, dimensions={0}, use_global_device_ids=true | all-gather | bytes 393216 | tf_op jit(solution)/shard_map/all_gather | solution.py:66
  55.8 1.0 %fusion.21 = f32[1,1,128,128]{3,2,1,0:T(8,128)} fusion(bf16[2,256,256]{2,1,0:T(8,128)(2,1)S(1)} %bitcast.51, bf16[128,2,256]{2,1,0:T(2,128)(2,1)S(1)} %reshape_squeeze.3), kind=kOutput, calls=%fused_computation.20 | convolution fusion | flops 50397184 | bytes 458752 | tf_op jit(solution)/shard_map/rnl,snl->rs/dot_general | solution.py:73
  56.8 6.0 %collective-permute-done = f32[768,768]{1,0:T(8,128)S(1)} collective-permute-done((f32[768,768]{1,0:T(8,128)}, f32[768,768]{1,0:T(8,128)S(1)}, u32[]{:S(2)}, u32[]{:S(2)}) %collective-permute-start) | collective-permute-done | bytes 2359328 | tf_op jit(solution)/shard_map/ppermute | solution.py:14
  62.8 6.9 %fusion.7 = f32[1,1,768,768]{3,2,1,0:T(8,128)} fusion(f32[768,768]{1,0:T(8,128)S(1)} %collective-permute-done, bf16[16,128,2048]{1,2,0:T(8,128)(2,1)} %convert_bitcast_fusion, bf16[16,128,2048]{1,2,0:T(8,128)(2,1)} %copy-done.1), kind=kOutput, calls=%fused_computation.11 | convolution fusion | flops 2417098752 | bytes 11010048 | tf_op jit(solution)/shard_map/kbi,kbj->ij/dot_general | solution.py:28
  (2 shorter events, 0.0 us)
Async XLA Ops:
  0.6 19.6 %copy-start = (bf16[1,1,16,128,128]{4,3,2,1,0:T(8,128)(2,1)S(1)}, bf16[1,1,16,128,128]{4,3,2,1,0:T(8,128)(2,1)}, u32[]{:S(2)}) copy-start(bf16[1,1,16,128,128]{4,3,2,1,0:T(8,128)(2,1)} %param.6) | copy-start | bytes 1572868
  0.6 13.0 %copy-start.3 = (s32[1,1,16,16]{3,2,1,0:T(8,128)S(1)}, s32[1,1,16,16]{3,2,1,0:T(8,128)}, u32[]{:S(2)}) copy-start(s32[1,1,16,16]{3,2,1,0:T(8,128)} %param.7) | copy-start | bytes 3076
  20.2 13.2 %copy-start.1 = (bf16[16,128,2048]{1,2,0:T(8,128)(2,1)}, bf16[16,128,2048]{1,2,0:T(8,128)(2,1)S(1)}, u32[]{:S(2)}) copy-start(bf16[16,128,2048]{1,2,0:T(8,128)(2,1)S(1)} %bitcast_multiply_fusion) | copy-start | bytes 25165828
  25.3 14.0 %copy-start.2 = (bf16[1,1,128,512]{3,2,1,0:T(8,128)(2,1)S(1)}, bf16[1,1,128,512]{3,2,1,0:T(8,128)(2,1)}, u32[]{:S(2)}) copy-start(bf16[1,1,128,512]{3,2,1,0:T(8,128)(2,1)} %param.9) | copy-start | bytes 393220
  31.5 31.3 %collective-permute-start = (f32[768,768]{1,0:T(8,128)}, f32[768,768]{1,0:T(8,128)S(1)}, u32[]{:S(2)}, u32[]{:S(2)}) collective-permute-start(f32[768,768]{1,0:T(8,128)} %bitcast_negate_fusion), channel_id=1, source_target_pairs={{0,1},{1,2},{2,3},{3,4},{4,5},{5,6},{6,7},{7,8},{8,9},{9,10},{10,1... | collective-permute-start | bytes 7077896 | tf_op jit(solution)/shard_map/ppermute | solution.py:14
  35.9 9.8 %collective-permute-start.1 = (f32[256,256]{1,0:T(8,128)}, f32[256,256]{1,0:T(8,128)S(1)}, u32[]{:S(2)}, u32[]{:S(2)}) collective-permute-start(f32[256,256]{1,0:T(8,128)} %fusion.16), channel_id=1, source_target_pairs={{0,16},{1,17},{2,18},{3,19},{4,20},{5,21},{6,22},{7,23},{8,24},{9,... | collective-permute-start | bytes 786440 | tf_op jit(solution)/shard_map/ppermute | solution.py:14
where the time goes:
time: 70.3 us; the launch traced here: 69.7 us
  matrix products  24.3 us (35%)
  local copies, waits for them, and re-layouts  12.5 us (18%)
  waiting for transfers between devices  12.4 us (18%)
  blocking collectives  7.37 us (10%)
  other arithmetic  6.46 us (9%)
  starting transfers between devices  5.33 us (8%)
  between operations  1.39 us (2%)
    dot_general x4, matrix products, edge_parts(): jnp.einsum('kbi,kbj->ij', slab, answer, preferred_element_type=jnp.float32)  18.2 us
    ppermute x2, waiting for transfers between devices, from_behind(): return lax.ppermute(block, axis, route)  12.4 us
    unnamed x9, local copies, waits for them, and re-layouts  12.4 us
    all_gather x1, blocking collectives, shards(): piece = lax.all_gather(front_half, 'ew', axis=0, tiled=True)  7.37 us
    mul x1, other arithmetic, shards(): masked = coupling * keep[:, None, :]  6.38 us
    ppermute x2, starting transfers between devices, from_behind(): return lax.ppermute(block, axis, route)  5.33 us
    dot_general x1, matrix products, solve_all(): jnp.einsum('kab,kbc->kac', inverse, slabs, preferred_element_type=jnp.flo...  5.05 us
  transfers between devices with their start and end apart: 2, of which 2 were waited for; matrix products, arithmetic and copies ran while one was open for 9% of the time, Pallas kernels for 0%

commit v1 on v0

v1 whole, which is shorter than its diff:
```python
import functools

import jax
import jax.numpy as jnp
from jax import lax
from jax.experimental import pallas as pl
from jax.experimental.pallas import tpu as pltpu
from jax.sharding import PartitionSpec as P

B = 128
SN = 6
SE = 2
T = 256
MESH = pl.DeviceIdType.MESH
TOP = 32767.0


def dot_tn(a, b):
    return lax.dot_general(a, b, (((0,), (0,)), ((), ())), preferred_element_type=jnp.float32)


def dot_nn(a, b):
    return lax.dot_general(a, b, (((1,), (0,)), ((), ())), preferred_element_type=jnp.float32)


def dot_nt(a, b):
    return lax.dot_general(a, b, (((1,), (1,)), ((), ())), preferred_element_type=jnp.float32)


def encode(block):
    top = jnp.maximum(jnp.max(jnp.abs(block), axis=0, keepdims=True), 2e-34)
    code = jnp.round(block * (TOP / top)).astype(jnp.int32).astype(jnp.int16)
    return code, top * (1.0 / TOP)


def decode(code, scale):
    return code.astype(jnp.int32).astype(jnp.float32) * scale


def kernel(
    n_ew, n_ns, depth,
    coup, inv, pat, cnt, bas,
    south, west, coarse,
    cm, am, qm, keep, solved,
    off_out, dia_out, sca_out, off_in, dia_in, sca_in,
    east_out, east_in, fronts,
    load_sem, send_sem, recv_sem, esend, erecv, gsend, grecv,
):
    e = lax.axis_index("ew")
    n = lax.axis_index("ns")
    has_next = n < n_ns - 1
    has_prev = n > 0
    north0 = SN * B
    west0 = 2 * SN * B
    east0 = west0 + SE * B
    stripes = SN * B // T

    barrier = pltpu.get_barrier_semaphore()

    @pl.when(has_prev)
    def _():
        pl.semaphore_signal(barrier, inc=1, device_id=(e, n - 1), device_id_type=MESH)

    @pl.when(has_next)
    def _():
        pl.semaphore_signal(barrier, inc=1, device_id=(e, n + 1), device_id_type=MESH)

    for d in range(1, n_ew):
        pl.semaphore_signal(
            barrier, inc=1, device_id=(lax.rem(e + d, n_ew), n), device_id_type=MESH
        )

    copies = {}

    def load(name, src, dst):
        copies[name] = pltpu.make_async_copy(src, dst, load_sem.at[len(copies)])
        copies[name].start()

    load("inv", inv, am)
    for name, start, width in (
        ("north", north0, SN * B),
        ("east", east0, SE * B),
        ("west", west0, SE * B),
        ("south", 0, SN * B),
    ):
        load(name, coup.at[:, pl.ds(start, width)], cm.at[:, pl.ds(start, width)])
    load("bas", bas, qm)

    blocks = pat.shape[1]
    lane = lax.broadcasted_iota(jnp.int32, (blocks, blocks * B), 1)
    row = lax.broadcasted_iota(jnp.int32, (blocks, blocks * B), 0)
    spread = jnp.where((lane >= row * B) & (lane < row * B + B), 1.0, 0.0).astype(jnp.bfloat16)
    live = lax.broadcasted_iota(jnp.int32, pat.shape, 0) < cnt[0, 0]
    touched = jnp.where(live, pat[...], 0).astype(jnp.float32).astype(jnp.bfloat16)
    keep[...] = dot_nn(touched, spread)

    @pl.when(n == 0)
    def _():
        off_in[...] = jnp.zeros_like(off_in)
        dia_in[...] = jnp.zeros_like(dia_in)
        sca_in[...] = jnp.zeros_like(sca_in)

    @pl.when(e == 0)
    def _():
        east_in[...] = jnp.zeros_like(east_in)

    def mask(start, width):
        for k in range(depth):
            rows = slice(k * B, k * B + B)
            cols = slice(start, start + width)
            cm[rows, cols] = cm[rows, cols] * keep[k : k + 1, cols].astype(jnp.bfloat16)

    def solve(start):
        for k in range(depth):
            rows = slice(k * B, k * B + B)
            solved[rows, :] = dot_nn(am[rows, :], cm[rows, start : start + T]).astype(jnp.bfloat16)

    def tile(start):
        return -dot_tn(cm[:, start : start + T], solved[...])

    def to_next(j):
        device = (e, n + 1)
        out = []
        sem = 3 * j
        if j < stripes - 1:
            first = j * (2 * stripes - 1 - j) // 2
            span = pl.ds(first, stripes - 1 - j)
            out.append((off_out.at[span], off_in.at[span], sem))
        out.append((dia_out.at[j], dia_in.at[j], sem + 1))
        out.append((sca_out.at[j], sca_in.at[j], sem + 2))
        return [
            pltpu.make_async_remote_copy(
                src_ref=s, dst_ref=d, send_sem=send_sem.at[m], recv_sem=recv_sem.at[m],
                device_id=device, device_id_type=MESH,
            )
            for s, d, m in out
        ]

    def north_stripe(j):
        solve(north0 + j * T)
        first = j * (2 * stripes - 1 - j) // 2
        for i in range(j + 1, stripes):
            code, scale = encode(tile(north0 + i * T))
            off_out[first + i - j - 1] = code
            sca_out[j, i - j - 1 : i - j, :] = scale
        t = tile(north0 + j * T)
        for b, (r, c) in enumerate(((0, 0), (1, 0), (1, 1))):
            code, scale = encode(t[r * B : r * B + B, c * B : c * B + B])
            dia_out[j, b * B : b * B + B, :] = code
            sca_out[j, 4 + b : 5 + b, 0:B] = scale
        if j == 0:
            peers = n_ew - 1 + has_prev.astype(jnp.int32) + has_next.astype(jnp.int32)
            pl.semaphore_wait(barrier, peers)

        @pl.when(has_next)
        def _():
            for c in to_next(j):
                c.start()

    sca_out[...] = jnp.zeros_like(sca_out)
    copies["inv"].wait()
    copies["north"].wait()
    mask(north0, SN * B)
    north_stripe(0)

    copies["east"].wait()
    mask(east0, SE * B)
    solve(east0)
    east_out[...] = tile(east0)
    east_copy = pltpu.make_async_remote_copy(
        src_ref=east_out, dst_ref=east_in, send_sem=esend, recv_sem=erecv,
        device_id=(e + 1, n), device_id_type=MESH,
    )

    @pl.when(e < n_ew - 1)
    def _():
        east_copy.start()

    for j in range(1, stripes):
        north_stripe(j)

    copies["west"].wait()
    mask(west0, SE * B)
    solve(west0)
    west[...] = tile(west0)

    copies["south"].wait()
    mask(0, SN * B)
    for j in range(stripes):
        solve(j * T)
        for i in range(j, stripes):
            south[i * T : i * T + T, j * T : j * T + T] = tile(i * T)

    @pl.when(e > 0)
    def _():
        east_copy.wait_recv()

    front = west[...] + east_in[...]
    west[...] = front
    fronts[e] = front.astype(jnp.bfloat16)

    def gather(d):
        return pltpu.make_async_remote_copy(
            src_ref=fronts.at[e], dst_ref=fronts.at[e], send_sem=gsend.at[d - 1],
            recv_sem=grecv.at[d - 1], device_id=(lax.rem(e + d, n_ew), n), device_id_type=MESH,
        )

    for d in range(1, n_ew):
        gather(d).start()

    def finish(j):
        @pl.when(has_prev)
        def _():
            for c in to_next(j):
                c.wait_recv()

        first = j * (2 * stripes - 1 - j) // 2
        cols = slice(j * T, j * T + T)
        for i in range(j + 1, stripes):
            rows = slice(i * T, i * T + T)
            scale = sca_in[j, i - j - 1 : i - j, :]
            total = south[rows, cols] + decode(off_in[first + i - j - 1], scale)
            south[rows, cols] = total
            south[cols, rows] = total.T
        o = j * T
        parts = [
            decode(dia_in[j, b * B : b * B + B, :], sca_in[j, 4 + b : 5 + b, 0:B]) for b in range(3)
        ]
        south[o : o + B, o : o + B] += parts[0]
        south[o + B : o + T, o + B : o + T] += parts[2]
        low = south[o + B : o + T, o : o + B] + parts[1]
        south[o + B : o + T, o : o + B] = low
        south[o : o + B, o + B : o + T] = low.T

    for j in range(stripes - 1):
        finish(j)

    copies["bas"].wait()
    total = jnp.zeros(coarse.shape, jnp.float32)
    for d in range(n_ew):
        if d > 0:
            gather(d).wait_recv()
        j = lax.rem(e + n_ew - d, n_ew)
        q = qm[:, pl.ds(pl.multiple_of(j * SE * B, SE * B), SE * B)]
        projected = dot_nn(q, fronts[j]).astype(jnp.bfloat16)
        total = total + dot_nt(projected, q)
    coarse[...] = total

    finish(stripes - 1)

    for d in range(1, n_ew):
        gather(d).wait_send()

    @pl.when(e < n_ew - 1)
    def _():
        east_copy.wait_send()

    @pl.when(has_next)
    def _():
        for j in range(stripes):
            for c in to_next(j):
                c.wait_send()


def shards(n_ew, n_ns, couplings, inverses, pattern, counts, basis):
    depth = couplings.shape[2]
    width = couplings.shape[4]
    coup = couplings.reshape(depth * B, width)
    inv = inverses.reshape(depth * B, B)
    pat = pattern[0, 0]
    bas = basis[0, 0]
    stripes = SN * B // T
    offs = stripes * (stripes - 1) // 2
    east = SE * B
    f32, bf16, i16 = jnp.float32, jnp.bfloat16, jnp.int16
    vmem = pl.BlockSpec(memory_space=pltpu.VMEM)
    anyspace = pl.BlockSpec(memory_space=pltpu.HBM)
    south, west, coarse = pl.pallas_call(
        functools.partial(kernel, n_ew, n_ns, depth),
        out_shape=(
            jax.ShapeDtypeStruct((SN * B, SN * B), f32),
            jax.ShapeDtypeStruct((east, east), f32),
            jax.ShapeDtypeStruct((bas.shape[0], bas.shape[0]), f32),
        ),
        in_specs=[anyspace, anyspace, vmem, pl.BlockSpec(memory_space=pltpu.SMEM), anyspace],
        out_specs=(vmem, vmem, vmem),
        scratch_shapes=[
            pltpu.VMEM((depth * B, width), bf16),
            pltpu.VMEM((depth * B, B), bf16),
            pltpu.VMEM(bas.shape, bf16),
            pltpu.VMEM((depth, width), f32),
            pltpu.VMEM((depth * B, T), bf16),
            pltpu.VMEM((offs, T, T), i16),
            pltpu.VMEM((stripes, 3 * B, B), i16),
            pltpu.VMEM((stripes, 8, T), f32),
            pltpu.VMEM((offs, T, T), i16),
            pltpu.VMEM((stripes, 3 * B, B), i16),
            pltpu.VMEM((stripes, 8, T), f32),
            pltpu.VMEM((east, east), f32),
            pltpu.VMEM((east, east), f32),
            pltpu.VMEM((n_ew, east, east), bf16),
            pltpu.SemaphoreType.DMA((6,)),
            pltpu.SemaphoreType.DMA((3 * stripes,)),
            pltpu.SemaphoreType.DMA((3 * stripes,)),
            pltpu.SemaphoreType.DMA,
            pltpu.SemaphoreType.DMA,
            pltpu.SemaphoreType.DMA((max(n_ew - 1, 1),)),
            pltpu.SemaphoreType.DMA((max(n_ew - 1, 1),)),
        ],
        compiler_params=pltpu.CompilerParams(
            collective_id=0, has_side_effects=True, vmem_limit_bytes=60 * 2**20
        ),
        cost_estimate=pl.CostEstimate(
            flops=5 * 10**9, bytes_accessed=12 * 10**6, transcendentals=0
        ),
        name="fronts",
    )(coup, inv, pat, counts, bas)
    return (south[None, None], west[None, None], coarse[None, None])


def solution(mesh):
    sizes = (mesh.shape["ew"], mesh.shape["ns"])
    return jax.shard_map(
        functools.partial(shards, *sizes),
        mesh=mesh,
        in_specs=(
            P("ew", "ns", None, None, None),
            P("ew", "ns", None, None, None),
            P("ew", "ns", None, None),
            P("ew", "ns"),
            P("ew", "ns", None, None),
        ),
        out_specs=(P("ew", "ns", None, None), P("ew", "ns", None, None), P("ew", "ns", None, None)),
        check_vma=False,
    )
```

time: 70.3 us -> 27 us (0.38)
  the two profiles are of different devices: /device:TPU:16 before, /device:TPU:0 now
where the time goes in v1:
time: 27 us; the launch traced here: 26.8 us
  Pallas kernels  20.9 us (77%)
  local copies, waits for them, and re-layouts  4.61 us (17%)
  between operations  1.3 us (5%)
    pallas_call x1, Pallas kernels, shards(): pl.pallas_call(functools.partial(kernel, n_ew, n_ns, depth), out_shape=(j...  20.9 us
    unnamed x7, local copies, waits for them, and re-layouts  4.61 us

profile of v1, /device:TPU:0, one launch (start us, length us, event | category | flops | bytes accessed | tf_op | source)
XLA Modules:
  0.0 26.8 jit_solution(5787834161752274015)
XLA Ops:
  1.3 20.9 %fronts.1 = (f32[768,768]{1,0:T(8,128)}, f32[256,256]{1,0:T(8,128)}, f32[128,128]{1,0:T(8,128)}) custom-call(bf16[2048,2048]{1,0:T(8,128)(2,1)} %bitcast.10, bf16[2048,128]{1,0:T(8,128)(2,1)} %bitcast.11, s32[16,16]{1,0:T(8,128)} %bitcast.13, s32[1,1]{1,0:T(1,128)S(6)} %copy.11.cnt, bf16[128,512]{1,0:T(8,128)(2,1)} %bitcast.12), custom_call_target="tpu_custom_call" | custom-call | flops 5000000000 | bytes 12000000 | tf_op jit(solution)/shard_map/fronts/pallas_call | solution.py:278
  22.2 0.0 copy-start
  22.2 0.0 copy-start.1
  22.2 3.3 %copy.12 = f32[1,1,768,768]{3,2,1,0:T(8,128)} copy(f32[1,1,768,768]{3,2,1,0:T(8,128)} %bitcast.7) | data formatting | bytes 4718592
  25.5 0.0 copy-done
  25.5 0.7 %copy.13 = f32[1,1,256,256]{3,2,1,0:T(8,128)} copy(f32[1,1,256,256]{3,2,1,0:T(8,128)S(1)} %bitcast.8) | data formatting | bytes 524288
  26.2 0.0 copy-done.1
  26.2 0.6 %copy.14 = f32[1,1,128,128]{3,2,1,0:T(8,128)} copy(f32[1,1,128,128]{3,2,1,0:T(8,128)S(1)} %bitcast.9) | data formatting | bytes 131072
Async XLA Ops:
  22.2 3.3 %copy-start = (f32[256,256]{1,0:T(8,128)S(1)}, f32[256,256]{1,0:T(8,128)}, u32[]{:S(2)}) copy-start(f32[256,256]{1,0:T(8,128)} %get-tuple-element.7) | copy-start | bytes 786436
  22.2 4.0 %copy-start.1 = (f32[128,128]{1,0:T(8,128)S(1)}, f32[128,128]{1,0:T(8,128)}, u32[]{:S(2)}) copy-start(f32[128,128]{1,0:T(8,128)} %get-tuple-element.8) | copy-start | bytes 196612

commit v2 on v1

--- a/solution.py
+++ b/solution.py
@@ -11,6 +11,7 @@
 SN = 6
 SE = 2
 T = 256
+XPOSE, WIDE, REMOTE = 'xlu', 1, 1
 MESH = pl.DeviceIdType.MESH
 TOP = 32767.0
 
@@ -41,7 +42,7 @@
     n_ew, n_ns, depth,
     coup, inv, pat, cnt, bas,
     south, west, coarse,
-    cm, am, qm, keep, solved,
+    cm, ct, am, qm, keep, solved,
     off_out, dia_out, sca_out, off_in, dia_in, sca_in,
     east_out, east_in, fronts,
     load_sem, send_sem, recv_sem, esend, erecv, gsend, grecv,
@@ -76,9 +77,18 @@
         copies[name] = pltpu.make_async_copy(src, dst, load_sem.at[len(copies)])
         copies[name].start()
 
-    load("inv", inv, am)
+    pairs = depth // 2
+    am[:, 0:B, B:T] = jnp.zeros((pairs, B, B), am.dtype)
+    am[:, B:T, 0:B] = jnp.zeros((pairs, B, B), am.dtype)
+    for p in range(2):
+        half = pl.ds(p * B, B)
+        load(("inv", p), inv.at[:, p], am.at[:, half, half])
+    parts = 4
+    span = depth * B // parts
+    for p in range(parts):
+        rows, cols = pl.ds(p * span, span), pl.ds(north0, SN * B)
+        load(("north", p), coup.at[rows, cols], cm.at[rows, cols])
     for name, start, width in (
-        ("north", north0, SN * B),
         ("east", east0, SE * B),
         ("west", west0, SE * B),
         ("south", 0, SN * B),
@@ -96,30 +106,47 @@
 
     @pl.when(n == 0)
     def _():
-        off_in[...] = jnp.zeros_like(off_in)
-        dia_in[...] = jnp.zeros_like(dia_in)
         sca_in[...] = jnp.zeros_like(sca_in)
 
-    @pl.when(e == 0)
-    def _():
-        east_in[...] = jnp.zeros_like(east_in)
-
-    def mask(start, width):
-        for k in range(depth):
-            rows = slice(k * B, k * B + B)
-            cols = slice(start, start + width)
-            cm[rows, cols] = cm[rows, cols] * keep[k : k + 1, cols].astype(jnp.bfloat16)
+    def turn(block):
+        if XPOSE == 'xlu':
+            return block.T
+        return dot_nt(eye, block).astype(jnp.bfloat16)
+
+    eye = (
+        lax.broadcasted_iota(jnp.int32, (T, T), 0) == lax.broadcasted_iota(jnp.int32, (T, T), 1)
+    ).astype(jnp.float32).astype(jnp.bfloat16)
+
+    def mask(start, width, first=0, last=depth):
+        for k in range(first, last, 2):
+            rows = slice(k * B, k * B + T)
+            for c in range(start, start + width, T):
+                cols = slice(c, c + T)
+                wide = jnp.concatenate(
+                    [jnp.broadcast_to(keep[k + p : k + p + 1, cols], (B, T)) for p in range(2)]
+                ).astype(jnp.bfloat16)
+                masked = cm[rows, cols] * wide
+                cm[rows, cols] = masked
+                ct[cols, rows] = turn(masked)
 
     def solve(start):
-        for k in range(depth):
-            rows = slice(k * B, k * B + B)
-            solved[rows, :] = dot_nn(am[rows, :], cm[rows, start : start + T]).astype(jnp.bfloat16)
+        for k in range(pairs):
+            rows = slice(k * T, k * T + T)
+            solved[rows, :] = dot_nn(am[k], cm[rows, start : start + T]).astype(jnp.bfloat16)
 
     def tile(start):
-        return -dot_tn(cm[:, start : start + T], solved[...])
+        return -dot_nn(ct[start : start + T, :], solved[...])
+
+    def tiles(start, end):
+        if WIDE:
+            whole = -dot_nn(ct[start:end, :], solved[...])
+            return [whole[o : o + T] for o in range(0, end - start, T)]
+        return [tile(o) for o in range(start, end, T)]
 
     def to_next(j):
         device = (e, n + 1)
+        if not REMOTE:
+            return []
         out = []
         sem = 3 * j
         if j < stripes - 1:
@@ -139,11 +166,12 @@
     def north_stripe(j):
         solve(north0 + j * T)
         first = j * (2 * stripes - 1 - j) // 2
+        results = tiles(north0 + j * T, north0 + SN * B)
         for i in range(j + 1, stripes):
-            code, scale = encode(tile(north0 + i * T))
+            code, scale = encode(results[i - j])
             off_out[first + i - j - 1] = code
             sca_out[j, i - j - 1 : i - j, :] = scale
-        t = tile(north0 + j * T)
+        t = results[0]
         for b, (r, c) in enumerate(((0, 0), (1, 0), (1, 1))):
             code, scale = encode(t[r * B : r * B + B, c * B : c * B + B])
             dia_out[j, b * B : b * B + B, :] = code
@@ -158,9 +186,11 @@
                 c.start()
 
     sca_out[...] = jnp.zeros_like(sca_out)
-    copies["inv"].wait()
-    copies["north"].wait()
-    mask(north0, SN * B)
+    for p in range(2):
+        copies["inv", p].wait()
+    for p in range(parts):
+        copies["north", p].wait()
+        mask(north0, SN * B, p * depth // parts, (p + 1) * depth // parts)
     north_stripe(0)
 
     copies["east"].wait()
@@ -188,14 +218,14 @@
     mask(0, SN * B)
     for j in range(stripes):
         solve(j * T)
-        for i in range(j, stripes):
-            south[i * T : i * T + T, j * T : j * T + T] = tile(i * T)
+        for i, result in enumerate(tiles(j * T, SN * B), j):
+            south[i * T : i * T + T, j * T : j * T + T] = result
 
     @pl.when(e > 0)
     def _():
         east_copy.wait_recv()
 
-    front = west[...] + east_in[...]
+    front = west[...] + jnp.where(e > 0, east_in[...], 0.0)
     west[...] = front
     fronts[e] = front.astype(jnp.bfloat16)
 
@@ -262,11 +292,22 @@
                 c.wait_send()
 
 
+def write_out(south_in, west_in, coarse_in, south, west, coarse, sems):
+    copies = [
+        pltpu.make_async_copy(a, b, sems.at[m])
+        for m, (a, b) in enumerate(((south_in, south), (west_in, west), (coarse_in, coarse)))
+    ]
+    for c in copies:
+        c.start()
+    for c in copies:
+        c.wait()
+
+
 def shards(n_ew, n_ns, couplings, inverses, pattern, counts, basis):
     depth = couplings.shape[2]
     width = couplings.shape[4]
     coup = couplings.reshape(depth * B, width)
-    inv = inverses.reshape(depth * B, B)
+    inv = inverses.reshape(depth // 2, 2, B, B)
     pat = pattern[0, 0]
     bas = basis[0, 0]
     stripes = SN * B // T
@@ -286,7 +327,8 @@
         out_specs=(vmem, vmem, vmem),
         scratch_shapes=[
             pltpu.VMEM((depth * B, width), bf16),
-            pltpu.VMEM((depth * B, B), bf16),
+            pltpu.VMEM((width, depth * B), bf16),
+            pltpu.VMEM((depth // 2, T, T), bf16),
             pltpu.VMEM(bas.shape, bf16),
             pltpu.VMEM((depth, width), f32),
             pltpu.VMEM((depth * B, T), bf16),
@@ -299,7 +341,7 @@
             pltpu.VMEM((east, east), f32),
             pltpu.VMEM((east, east), f32),
             pltpu.VMEM((n_ew, east, east), bf16),
-            pltpu.SemaphoreType.DMA((6,)),
+            pltpu.SemaphoreType.DMA((10,)),
             pltpu.SemaphoreType.DMA((3 * stripes,)),
             pltpu.SemaphoreType.DMA((3 * stripes,)),
             pltpu.SemaphoreType.DMA,
@@ -308,13 +350,23 @@
             pltpu.SemaphoreType.DMA((max(n_ew - 1, 1),)),
         ],
         compiler_params=pltpu.CompilerParams(
-            collective_id=0, has_side_effects=True, vmem_limit_bytes=60 * 2**20
+            collective_id=0, has_side_effects=True, vmem_limit_bytes=50 * 2**20
         ),
         cost_estimate=pl.CostEstimate(
             flops=5 * 10**9, bytes_accessed=12 * 10**6, transcendentals=0
         ),
         name="fronts",
     )(coup, inv, pat, counts, bas)
+    whole = (south, west, coarse)
+    south, west, coarse = pl.pallas_call(
+        write_out,
+        out_shape=[jax.ShapeDtypeStruct(x.shape, x.dtype) for x in whole],
+        in_specs=[pl.BlockSpec(memory_space=pltpu.VMEM)] * 3,
+        compiler_params=pltpu.CompilerParams(vmem_limit_bytes=4 * 2**20),
+        out_specs=[pl.BlockSpec(memory_space=pltpu.HBM)] * 3,
+        scratch_shapes=[pltpu.SemaphoreType.DMA((3,))],
+        name="write_out",
+    )(*whole)
     return (south[None, None], west[None, None], coarse[None, None])
 
 

time: 27 us -> 25.6 us (0.948)
  local copies, waits for them, and re-layouts: 4.61 us -> 2.63 us
  Pallas kernels: 20.9 us -> 21.4 us
    unnamed x7 -> x6, local copies, waits for them, and re-layouts: 4.61 us -> 2.63 us
    pallas_call x0 -> x1, Pallas kernels: none -> 1.52 us  [shards(): pl.pallas_call(write_out, out_shape=[jax.ShapeDtypeStruct(x.shape, x.dtyp...]
    pallas_call x1, Pallas kernels: 20.9 us -> 19.9 us  [shards(): pl.pallas_call(functools.partial(kernel, n_ew, n_ns, depth), out_shape=(j...]
where the time goes in v2:
time: 25.6 us; the launch traced here: 25.3 us
  Pallas kernels  21.4 us (84%)
  local copies, waits for them, and re-layouts  2.63 us (10%)
  between operations  1.3 us (5%)
    pallas_call x1, Pallas kernels, shards(): pl.pallas_call(functools.partial(kernel, n_ew, n_ns, depth), out_shape=(j...  19.9 us
    unnamed x6, local copies, waits for them, and re-layouts  2.63 us
    pallas_call x1, Pallas kernels, shards(): pl.pallas_call(write_out, out_shape=[jax.ShapeDtypeStruct(x.shape, x.dtyp...  1.52 us

profile of v2, /device:TPU:0, one launch (start us, length us, event | category | flops | bytes accessed | tf_op | source)
XLA Modules:
  0.0 25.3 jit_solution(14392747943658607442)
XLA Ops:
  1.3 0.0 copy-start
  1.3 1.0 %copy-done = bf16[1,1,16,128,128]{4,3,2,1,0:T(8,128)(2,1)S(1)} copy-done((bf16[1,1,16,128,128]{4,3,2,1,0:T(8,128)(2,1)S(1)}, bf16[1,1,16,128,128]{4,3,2,1,0:T(8,128)(2,1)}, u32[]{:S(2)}) %copy-start) | copy-done | bytes 524312
  2.3 0.0 copy-start.1
  2.3 0.9 %copy-done.1 = bf16[1,1,128,512]{3,2,1,0:T(8,128)(2,1)S(1)} copy-done((bf16[1,1,128,512]{3,2,1,0:T(8,128)(2,1)S(1)}, bf16[1,1,128,512]{3,2,1,0:T(8,128)(2,1)}, u32[]{:S(2)}) %copy-start.1) | copy-done | bytes 131096
  3.2 0.0 copy-start.2
  3.2 0.7 %copy-done.2 = s32[1,1,16,16]{3,2,1,0:T(8,128)S(1)} copy-done((s32[1,1,16,16]{3,2,1,0:T(8,128)S(1)}, s32[1,1,16,16]{3,2,1,0:T(8,128)}, u32[]{:S(2)}) %copy-start.2) | copy-done | bytes 1048
  3.9 19.9 %fronts.1 = (f32[768,768]{1,0:T(8,128)S(1)}, f32[256,256]{1,0:T(8,128)S(1)}, f32[128,128]{1,0:T(8,128)S(1)}) custom-call(bf16[2048,2048]{1,0:T(8,128)(2,1)} %bitcast.10, bf16[8,2,128,128]{3,2,1,0:T(8,128)(2,1)S(1)} %bitcast.7, s32[16,16]{1,0:T(8,128)S(1)} %bitcast.9, s32[1,1]{1,0:T(1,128)S(6)} %copy.8.cnt, bf16[128,512]{1,0:T(8,128)(2,1)S(1)} %bitcast.8), custom_call_target="tpu_custom_call" | custom-call | flops 5000000000 | bytes 12000000 | tf_op jit(solution)/shard_map/fronts/pallas_call | solution.py:319
  23.8 1.5 %write_out.1 = (f32[768,768]{1,0:T(8,128)}, f32[256,256]{1,0:T(8,128)}, f32[128,128]{1,0:T(8,128)}) custom-call(f32[768,768]{1,0:T(8,128)S(1)} %get-tuple-element.9.south_in, f32[256,256]{1,0:T(8,128)S(1)} %get-tuple-element.10.west_in, f32[128,128]{1,0:T(8,128)S(1)} %get-tuple-element.11.coarse_in), custom_call_target="tpu_custom_call" | custom-call | tf_op jit(solution)/shard_map/write_out/pallas_call | solution.py:361
Async XLA Ops:
  1.3 1.0 %copy-start = (bf16[1,1,16,128,128]{4,3,2,1,0:T(8,128)(2,1)S(1)}, bf16[1,1,16,128,128]{4,3,2,1,0:T(8,128)(2,1)}, u32[]{:S(2)}) copy-start(bf16[1,1,16,128,128]{4,3,2,1,0:T(8,128)(2,1)} %param.6) | copy-start | bytes 1572868
  2.3 0.9 %copy-start.1 = (bf16[1,1,128,512]{3,2,1,0:T(8,128)(2,1)S(1)}, bf16[1,1,128,512]{3,2,1,0:T(8,128)(2,1)}, u32[]{:S(2)}) copy-start(bf16[1,1,128,512]{3,2,1,0:T(8,128)(2,1)} %param.9) | copy-start | bytes 393220
  3.2 0.7 %copy-start.2 = (s32[1,1,16,16]{3,2,1,0:T(8,128)S(1)}, s32[1,1,16,16]{3,2,1,0:T(8,128)}, u32[]{:S(2)}) copy-start(s32[1,1,16,16]{3,2,1,0:T(8,128)} %param.7) | copy-start | bytes 3076
